TPU v7x, 32 devices: a whole 2x2x4 slice. The times are simulated.
32 devices in a mesh: section: 4 (over z), row: 2 (over x), col: 4 (over y, core).
Axes of the slice: x: 2, y: 2, z: 4, core: 2. Of those that a mesh axis runs over, the one named last changes fastest.
Arguments:
- tokens: bfloat16 [4, 512, 4096], P('section', 'col', 'row'), may hold values from -6 to 6
- cotangent: bfloat16 [4, 512, 4096], P('section', 'col', 'row'), may hold values from -6 to 6
- noised: int32 [4, 512], P('section', 'col'), may hold values from 0 to 1, as said below
- gate_weight: bfloat16 [4, 4096, 16384], P('section', None, ('row', 'col')), may hold values from -0.09375 to 0.09375
- up_weight: bfloat16 [4, 4096, 16384], P('section', None, ('row', 'col')), may hold values from -0.09375 to 0.09375
- down_weight: bfloat16 [4, 16384, 4096], P('section', ('row', 'col')), may hold values from -0.046875 to 0.046875
- block_keep: int32 [4, 3, 32, 128], P('section', None, None, ('row', 'col')), may hold values 0 or 1
Outputs:
- grad_gate: bfloat16 [4, 4096, 16384], P('section', None, ('row', 'col'))
- grad_up: bfloat16 [4, 4096, 16384], P('section', None, ('row', 'col'))
- grad_down: bfloat16 [4, 16384, 4096], P('section', ('row', 'col'))
- handoff: bfloat16 [4, 512, 4096], P('section', 'col')
Inputs may be any that keep to these rules, and one draw needn't show every extreme that they name: Each aligned block of 128 tokens of a section (the tokens of one grid column) holds 1 to 96 noised tokens; in every section some block holds exactly 96.
All inputs are finite; a program needn't handle non-finite values. No bound on the sum of `block_keep` on one device may be relied on, other than what follows from the above.
Results may differ from a plain program's by a relative error of at most 0.0051.
Values may be sent and summed in bfloat16 or wider, within the bound.
A program may use at most 256 MiB of HBM per device.

v0:
```python
import jax
import jax.numpy as jnp
from jax import lax
from jax.experimental import pallas as pl
from jax.experimental.pallas import tpu as pltpu
from jax.sharding import PartitionSpec as P

CAP = 96
EDGE = 128
SUB = 16
VMEM = 44 * 1024 * 1024


def dot(left, right, left_dim, right_dim):
    return lax.dot_general(
        left,
        right,
        (((left_dim,), (right_dim,)), ((), ())),
        preferred_element_type=jnp.float32,
    )


def masked(values, mask):
    blocks, _, cols = mask.shape
    split = values.reshape(blocks, EDGE // SUB, SUB, cols)
    return (split * mask[:, None]).reshape(blocks * EDGE, cols)


def forward_kernel(tokens, gate, up, gate_mask, up_mask, gate_pre, up_pre):
    held = tokens[...]
    gate_pre[...] = dot(held, masked(gate[...], gate_mask[...]), 1, 0)
    up_pre[...] = dot(held, masked(up[...], up_mask[...]), 1, 0)


def middle_kernel(cot, down, down_mask, gate_pre, up_pre, hidden, grad_gate_pre, grad_up_pre):
    grad_hidden = dot(cot[...], masked(down[...], down_mask[...]), 1, 1)
    pre, up = gate_pre[...], up_pre[...]
    sigmoid = jax.nn.sigmoid(pre)
    silu = pre * sigmoid
    hidden[...] = (silu * up).astype(jnp.bfloat16)
    grad_gate_pre[...] = (grad_hidden * up * sigmoid * (1.0 + pre * (1.0 - sigmoid))).astype(
        jnp.bfloat16
    )
    grad_up_pre[...] = (grad_hidden * silu).astype(jnp.bfloat16)


def input_kernel(grad_gate_pre, grad_up_pre, gate, up, gate_mask, up_mask, out):
    total = dot(grad_gate_pre[...], masked(gate[...], gate_mask[...]), 1, 1)
    total += dot(grad_up_pre[...], masked(up[...], up_mask[...]), 1, 1)
    out[...] = total.astype(jnp.bfloat16)


def outer_kernel(left, right, mask, out):
    cols = right.shape[1]
    step = min(cols, 512)
    flipped = left[...].T
    for start in range(0, cols, step):
        part = pl.ds(start, step)
        product = dot(flipped, right[:, part], 1, 0).astype(jnp.bfloat16)
        out[:, part] = masked(product, mask[:, :, part])


def call(kernel, name, grid, ins, outs, flops, args):
    moved = sum(a.size * a.dtype.itemsize for a in args) + sum(
        s.size * s.dtype.itemsize for s, _ in outs
    )
    single = len(outs) == 1
    shapes = [s for s, _ in outs]
    specs = [b for _, b in outs]
    return pl.pallas_call(
        kernel,
        name=name,
        grid=(grid,),
        in_specs=ins,
        out_shape=shapes[0] if single else shapes,
        out_specs=specs[0] if single else specs,
        compiler_params=pltpu.CompilerParams(vmem_limit_bytes=VMEM),
        cost_estimate=pl.CostEstimate(flops=flops, bytes_accessed=moved, transcendentals=0),
    )(*args)


def whole_of(array):
    return pl.BlockSpec(array.shape, lambda i: (0,) * array.ndim)


def forward(tokens, gate, up, gate_mask, up_mask):
    rows, width = tokens.shape
    units = gate.shape[1]
    tile = min(256, units)
    weight = pl.BlockSpec((width, tile), lambda i: (0, i))
    mask = pl.BlockSpec((width // EDGE, SUB, tile), lambda i: (0, 0, i))
    out = (
        jax.ShapeDtypeStruct((rows, units), jnp.float32),
        pl.BlockSpec((rows, tile), lambda i: (0, i)),
    )
    return call(
        forward_kernel, "forward", units // tile,
        [whole_of(tokens), weight, weight, mask, mask], [out, out],
        4 * rows * width * units, (tokens, gate, up, gate_mask, up_mask),
    )


def middle(cot, down, down_mask, gate_pre, up_pre):
    rows, width = cot.shape
    units = down.shape[0]
    tile = min(256, units)
    columns = pl.BlockSpec((rows, tile), lambda i: (0, i))
    out = (jax.ShapeDtypeStruct((rows, units), jnp.bfloat16), columns)
    return call(
        middle_kernel, "middle", units // tile,
        [
            whole_of(cot),
            pl.BlockSpec((tile, width), lambda i: (i, 0)),
            pl.BlockSpec((tile // EDGE, SUB, width), lambda i: (i, 0, 0)),
            columns,
            columns,
        ],
        [out, out, out],
        2 * rows * width * units, (cot, down, down_mask, gate_pre, up_pre),
    )


def input_part(grad_gate_pre, grad_up_pre, gate, up, gate_mask, up_mask, part, parts):
    rows, units = grad_gate_pre.shape
    width = gate.shape[0] // parts
    tile = min(512, width)
    first = part * width // tile
    weight = pl.BlockSpec((tile, units), lambda i: (i + first, 0))
    mask = pl.BlockSpec((tile // EDGE, SUB, units), lambda i: (i + first, 0, 0))
    out = (
        jax.ShapeDtypeStruct((rows, width), jnp.bfloat16),
        pl.BlockSpec((rows, tile), lambda i: (0, i)),
    )
    return call(
        input_kernel, "input_part", width // tile,
        [whole_of(grad_gate_pre), whole_of(grad_up_pre), weight, weight, mask, mask], [out],
        4 * rows * width * units,
        (grad_gate_pre, grad_up_pre, gate, up, gate_mask, up_mask),
    )


def outer(left, right, mask, name):
    rows, height = left.shape
    cols = right.shape[1]
    tile = max(EDGE, min(height, 1024 * 1024 // cols))
    out = (
        jax.ShapeDtypeStruct((height, cols), jnp.bfloat16),
        pl.BlockSpec((tile, cols), lambda i: (i, 0)),
    )
    return call(
        outer_kernel, name, height // tile,
        [
            pl.BlockSpec((rows, tile), lambda i: (0, i)),
            whole_of(right),
            pl.BlockSpec((tile // EDGE, SUB, cols), lambda i: (i, 0, 0)),
        ],
        [out], 2 * rows * height * cols, (left, right, mask),
    )


def expand(keep):
    rows, cols = keep.shape
    wide = jnp.broadcast_to(
        keep.astype(jnp.bfloat16)[:, None, :, None], (rows, SUB, cols, EDGE)
    )
    return wide.reshape(rows, SUB, cols * EDGE)


def shifted(array, axis, by):
    peers = lax.axis_size(axis)
    pairs = [(i, i + by) for i in range(peers) if 0 <= i + by < peers]
    return lax.ppermute(array, axis, pairs)


def swap(array, axis, bit):
    return lax.ppermute(array, axis, [(i, i ^ bit) for i in range(lax.axis_size(axis))])


def select_rows(noised):
    slot = jnp.cumsum(noised) - 1
    return (
        (slot[None, :] == jnp.arange(CAP)[:, None]) & (noised[None, :] > 0)
    ).astype(jnp.bfloat16)


def side_by_side(own, other):
    first = lax.axis_index("row") == 0
    return jnp.concatenate(
        [jnp.where(first, own, other), jnp.where(first, other, own)], axis=-1
    )


def gather_pairs(own):
    half = own.shape[0] // 2
    top, bottom = own[:half], own[half:]
    top_x = swap(top, "row", 1)
    bottom_y = swap(bottom, "col", 2)
    top_wide = side_by_side(top, top_x)
    bottom_both = jnp.stack([bottom, bottom_y])
    top_y = swap(top_wide, "col", 2)
    bottom_x = swap(bottom_both, "row", 1)
    top_both = jnp.stack([top_wide, top_y])
    bottom_wide = side_by_side(bottom_both, bottom_x)
    top_core = swap(top_both, "col", 1)
    bottom_core = swap(bottom_wide, "col", 1)
    parts = [
        piece
        for y in range(2)
        for pair in ((top_both, bottom_wide), (top_core, bottom_core))
        for piece in (pair[0][y], pair[1][y])
    ]
    return jnp.concatenate(parts, axis=0)


def add(left, right):
    return (left.astype(jnp.float32) + right.astype(jnp.float32)).astype(jnp.bfloat16)


def by_row(block):
    half = block.shape[1] // 2
    first = lax.axis_index("row") == 0
    top, bottom = block[:, :half], block[:, half:]
    return jnp.where(first, top, bottom), jnp.where(first, bottom, top)


def scatter_pairs(left, right):
    def core(block):
        block = block.reshape(2, 2, CAP, block.shape[1])
        return add(block[:, 0], swap(block[:, 1], "col", 1))

    left, right = core(left), core(right)
    left = add(left[:1], swap(left[1:], "col", 2))
    keep, send = by_row(right)
    right = add(keep, swap(send, "row", 1))
    keep, send = by_row(left)
    left = add(keep, swap(send, "row", 1))[0]
    right = add(right[0], swap(right[1], "col", 2))
    return left, right


def on_device(tokens, cotangent, noised, gate_weight, up_weight, down_weight, block_keep):
    rows, cols = lax.axis_size("row"), lax.axis_size("col")
    paired = rows == 2 and cols == 4
    local_noised = noised[0]
    gate, up, down = gate_weight[0], up_weight[0], down_weight[0]
    gate_mask = expand(block_keep[0, 0])
    up_mask = expand(block_keep[0, 1])
    down_mask = expand(block_keep[0, 2].T)
    selector = select_rows(local_noised)
    next_selector = select_rows(shifted(local_noised, "section", -1))
    sent_tokens = dot(selector, tokens[0], 1, 0).astype(jnp.bfloat16)
    masked_cot = cotangent[0] * local_noised[:, None].astype(jnp.bfloat16)
    sent_cot = dot(selector, masked_cot, 1, 0).astype(jnp.bfloat16)

    def gather(block):
        wide = lax.all_gather(block, "row", axis=1, tiled=True)
        wide = wide.reshape(rows, CAP // rows, wide.shape[1])
        wide = lax.all_gather(wide, "col", axis=1, tiled=True)
        return wide.reshape(cols * CAP, wide.shape[2])

    if paired:
        all_tokens = gather_pairs(sent_tokens)
        sent_cot, _ = lax.optimization_barrier((sent_cot, all_tokens))
        all_cot = gather_pairs(sent_cot)
    else:
        all_tokens, all_cot = gather(sent_tokens), gather(sent_cot)
    gate_pre, up_pre = forward(all_tokens, gate, up, gate_mask, up_mask)
    hidden, grad_gate_pre, grad_up_pre = middle(all_cot, down, down_mask, gate_pre, up_pre)
    halves = [
        input_part(grad_gate_pre, grad_up_pre, gate, up, gate_mask, up_mask, part, 2)
        for part in range(2)
    ]
    grad_down = outer(hidden, all_cot, down_mask, "grad_down")
    grad_gate = outer(all_tokens, grad_gate_pre, gate_mask, "grad_gate")
    grad_up = outer(all_tokens, grad_up_pre, up_mask, "grad_up")
    if paired:
        pieces = [shifted(piece, "section", -1) for piece in scatter_pairs(*halves)]
        first = lax.axis_index("row") == 0
        blocks = []
        for piece in pieces:
            other = swap(piece, "row", 1)
            blocks.append(
                jnp.concatenate([jnp.where(first, piece, other), jnp.where(first, other, piece)])
            )
        block = jnp.concatenate(blocks, axis=1)
    else:
        share = lax.psum_scatter(
            jnp.concatenate(halves, axis=1).astype(jnp.float32),
            ("row", "col"),
            scatter_dimension=0,
            tiled=True,
        ).astype(jnp.bfloat16)
        share = shifted(share, "section", -1)
        block = lax.all_gather(share, "row", axis=0, tiled=True)
    handoff = dot(next_selector, block, 0, 0).astype(jnp.bfloat16)
    return (grad_gate[None], grad_up[None], grad_down[None], handoff[None])


def solution(mesh):
    placed = (
        P("section", "col", "row"),
        P("section", "col", "row"),
        P("section", "col"),
        P("section", None, ("row", "col")),
        P("section", None, ("row", "col")),
        P("section", ("row", "col"), None),
        P("section", None, None, ("row", "col")),
    )
    return jax.shard_map(
        on_device,
        mesh=mesh,
        in_specs=placed,
        out_specs=(
            P("section", None, ("row", "col")),
            P("section", None, ("row", "col")),
            P("section", ("row", "col"), None),
            P("section", "col", None),
        ),
        check_vma=False,
    )
```

profile of v0, /device:TPU:0, one launch (start us, length us, event | category | flops | bytes accessed | tf_op | source)
XLA Modules:
  0.0 190.5 jit_solution(6912511950525905571)
XLA Ops:
  4.1 3.0 %collective-permute-start = (bf16[48,2048]{1,0:T(8,128)(2,1)S(1)}, bf16[48,2048]{1,0:T(8,128)(2,1)S(1)}, u32[]{:S(2)}, u32[]{:S(2)}) collective-permute-start(bf16[48,2048]{1,0:T(8,128)(2,1)S(1)} %slice.127), channel_id=1, source_target_pairs={{0,4},{4,0},{1,5},{5,1},{2,6},{6,2},{3,7},{7,3},{8,12},{12,8},{9,1... | collective-permute-start | bytes 589832 | tf_op jit(solution)/shard_map/ppermute | solution.py:176
  9.9 2.1 %collective-permute-done = bf16[48,2048]{1,0:T(8,128)(2,1)S(1)} collective-permute-done((bf16[48,2048]{1,0:T(8,128)(2,1)S(1)}, bf16[48,2048]{1,0:T(8,128)(2,1)S(1)}, u32[]{:S(2)}, u32[]{:S(2)}) %collective-permute-start) | collective-permute-done | bytes 196640 | tf_op jit(solution)/shard_map/ppermute | solution.py:176
  12.8 1.8 collective-permute-start.1
  21.8 1.6 reduce-window.17
  25.4 1.8 collective-permute-start.2
  28.9 6.3 %collective-permute-done.2 = bf16[2,48,2048]{2,1,0:T(8,128)(2,1)S(1)} collective-permute-done((bf16[2,48,2048]{2,1,0:T(8,128)(2,1)S(1)}, bf16[2,48,2048]{2,1,0:T(8,128)(2,1)S(1)}, u32[]{:S(2)}, u32[]{:S(2)}) %collective-permute-start.2) | collective-permute-done | bytes 393248 | tf_op jit(solution)/shard_map/ppermute | solution.py:176
  36.5 2.2 %collective-permute-done.5 = bf16[2,48,4096]{2,1,0:T(8,128)(2,1)S(1)} collective-permute-done((bf16[2,48,4096]{2,1,0:T(8,128)(2,1)S(1)}, bf16[2,48,4096]{2,1,0:T(8,128)(2,1)S(1)}, u32[]{:S(2)}, u32[]{:S(2)}) %collective-permute-start.5) | collective-permute-done | bytes 786464 | tf_op jit(solution)/shard_map/ppermute | solution.py:176
  42.1 4.9 %collective-permute-done.6 = bf16[48,2048]{1,0:T(8,128)(2,1)S(1)} collective-permute-done((bf16[48,2048]{1,0:T(8,128)(2,1)S(1)}, bf16[48,2048]{1,0:T(8,128)(2,1)S(1)}, u32[]{:S(2)}, u32[]{:S(2)}) %collective-permute-start.6) | collective-permute-done | bytes 196640 | tf_op jit(solution)/shard_map/ppermute | solution.py:176
  47.0 1.5 collective-permute-start.7
  49.8 20.8 %forward.1 = (f32[384,2048]{1,0:T(8,128)S(1)}, f32[384,2048]{1,0:T(8,128)}) custom-call(bf16[384,4096]{1,0:T(8,128)(2,1)} %copy-done.5, bf16[4096,2048]{1,0:T(8,128)(2,1)} %bitcast.137, bf16[4096,2048]{1,0:T(8,128)(2,1)} %bitcast.140, bf16[32,16,2048]{2,1,0:T(8,128)(2,1)S(1)} %broadcast_in_dim.52.gate_mask.mask, ...), custom_call_target="tpu_custom_call" | custom-call | flops 12884901888 | bytes 47185920 | tf_op jit(solution)/shard_map/forward/pallas_call | solution.py:70
  72.4 8.2 %collective-permute-done.8 = bf16[2,48,2048]{2,1,0:T(8,128)(2,1)S(1)} collective-permute-done((bf16[2,48,2048]{2,1,0:T(8,128)(2,1)S(1)}, bf16[2,48,2048]{2,1,0:T(8,128)(2,1)S(1)}, u32[]{:S(2)}, u32[]{:S(2)}) %collective-permute-start.8) | collective-permute-done | bytes 393248 | tf_op jit(solution)/shard_map/ppermute | solution.py:176
  80.8 2.2 %collective-permute-done.11 = bf16[2,48,4096]{2,1,0:T(8,128)(2,1)S(1)} collective-permute-done((bf16[2,48,4096]{2,1,0:T(8,128)(2,1)S(1)}, bf16[2,48,4096]{2,1,0:T(8,128)(2,1)S(1)}, u32[]{:S(2)}, u32[]{:S(2)}) %collective-permute-start.11) | collective-permute-done | bytes 786464 | tf_op jit(solution)/shard_map/ppermute | solution.py:176
  83.5 14.0 %middle.1 = (bf16[384,2048]{1,0:T(8,128)(2,1)S(1)}, bf16[384,2048]{1,0:T(8,128)(2,1)S(1)}, bf16[384,2048]{1,0:T(8,128)(2,1)S(1)}) custom-call(bf16[384,4096]{1,0:T(8,128)(2,1)S(1)} %fusion.23.cot.right, bf16[2048,4096]{1,0:T(8,128)(2,1)} %bitcast.143, bf16[16,16,4096]{2,1,0:T(8,128)(2,1)S(1)} %broadcast_in_dim.49.down_mask.mask, f32[384,2048]{1,0:T(8,128)} %copy-done.4, ...), custom_call_target="tpu_custom_call" | custom-call | flops 6442450944 | bytes 33030144 | tf_op jit(solution)/shard_map/middle/pallas_call | solution.py:70
  97.5 10.1 %input_part.3 = bf16[384,2048]{1,0:T(8,128)(2,1)S(1)} custom-call(bf16[384,2048]{1,0:T(8,128)(2,1)S(1)} %get-tuple-element.13.right.grad_gate_pre, bf16[384,2048]{1,0:T(8,128)(2,1)S(1)} %get-tuple-element.14.right.grad_up_pre, bf16[4096,2048]{1,0:T(8,128)(2,1)} %bitcast.138, bf16[4096,2048]{1,0:T(8,128)(2,1)} %bitcast.141, ...), custom_call_target="tpu_custom_call" | custom-call | flops 6442450944 | bytes 42467328 | tf_op jit(solution)/shard_map/input_part/pallas_call | solution.py:70
  107.6 10.2 %input_part.2 = bf16[384,2048]{1,0:T(8,128)(2,1)S(1)} custom-call(bf16[384,2048]{1,0:T(8,128)(2,1)S(1)} %get-tuple-element.13.right.grad_gate_pre, bf16[384,2048]{1,0:T(8,128)(2,1)S(1)} %get-tuple-element.14.right.grad_up_pre, bf16[4096,2048]{1,0:T(8,128)(2,1)} %bitcast.139, bf16[4096,2048]{1,0:T(8,128)(2,1)} %bitcast.142, ...), custom_call_target="tpu_custom_call" | custom-call | flops 6442450944 | bytes 42467328 | tf_op jit(solution)/shard_map/input_part/pallas_call | solution.py:70
  117.9 12.0 %grad_up.1 = bf16[4096,2048]{1,0:T(8,128)(2,1)} custom-call(bf16[384,4096]{1,0:T(8,128)(2,1)S(1)} %copy-done.6, bf16[384,2048]{1,0:T(8,128)(2,1)S(1)} %get-tuple-element.14.right.grad_up_pre, bf16[32,16,2048]{2,1,0:T(8,128)(2,1)S(1)} %broadcast_in_dim.55.up_mask.mask), custom_call_target="tpu_custom_call" | custom-call | flops 6442450944 | bytes 23592960 | tf_op jit(solution)/shard_map/grad_up/pallas_call | solution.py:70
  130.6 12.0 %grad_gate.1 = bf16[4096,2048]{1,0:T(8,128)(2,1)} custom-call(bf16[384,4096]{1,0:T(8,128)(2,1)S(1)} %copy-done.6, bf16[384,2048]{1,0:T(8,128)(2,1)S(1)} %get-tuple-element.13.right.grad_gate_pre, bf16[32,16,2048]{2,1,0:T(8,128)(2,1)S(1)} %broadcast_in_dim.52.gate_mask.mask), custom_call_target="tpu_custom_call" | custom-call | flops 6442450944 | bytes 23592960 | tf_op jit(solution)/shard_map/grad_gate/pallas_call | solution.py:70
  144.7 1.6 collective-permute-start.14
  146.3 7.8 %collective-permute-done.19 = bf16[2,48,2048]{2,1,0:T(8,128)(2,1)S(1)} collective-permute-done((bf16[2,48,2048]{2,1,0:T(8,128)(2,1)S(1)}, bf16[2,48,2048]{2,1,0:T(8,128)(2,1)S(1)}, u32[]{:S(2)}, u32[]{:S(2)}) %collective-permute-start.19) | collective-permute-done | bytes 393248 | tf_op jit(solution)/shard_map/ppermute | solution.py:176
  156.0 1.5 collective-permute-start.15
  157.5 3.0 %collective-permute-done.20 = bf16[48,2048]{1,0:T(8,128)(2,1)S(1)} collective-permute-done((bf16[48,2048]{1,0:T(8,128)(2,1)S(1)}, bf16[48,2048]{1,0:T(8,128)(2,1)S(1)}, u32[]{:S(2)}, u32[]{:S(2)}) %collective-permute-start.20) | collective-permute-done | bytes 196640 | tf_op jit(solution)/shard_map/ppermute | solution.py:176
  163.2 6.8 %collective-permute-done.21 = bf16[48,2048]{1,0:T(8,128)(2,1)S(1)} collective-permute-done((bf16[48,2048]{1,0:T(8,128)(2,1)S(1)}, bf16[48,2048]{1,0:T(8,128)(2,1)S(1)}, u32[]{:S(2)}, u32[]{:S(2)}) %collective-permute-start.21) | collective-permute-done | bytes 196640 | tf_op jit(solution)/shard_map/ppermute | solution.py:172
  171.5 11.9 %grad_down.1 = bf16[2048,4096]{1,0:T(8,128)(2,1)} custom-call(bf16[384,2048]{1,0:T(8,128)(2,1)S(1)} %get-tuple-element.15.left, bf16[384,4096]{1,0:T(8,128)(2,1)S(1)} %copy-done.3, bf16[16,16,4096]{2,1,0:T(8,128)(2,1)S(1)} %broadcast_in_dim.49.down_mask.mask), custom_call_target="tpu_custom_call" | custom-call | flops 6442450944 | bytes 23592960 | tf_op jit(solution)/shard_map/grad_down/pallas_call | solution.py:70
  184.1 5.0 %collective-permute-done.17 = bf16[48,2048]{1,0:T(8,128)(2,1)S(1)} collective-permute-done((bf16[48,2048]{1,0:T(8,128)(2,1)S(1)}, bf16[48,2048]{1,0:T(8,128)(2,1)S(1)}, u32[]{:S(2)}, u32[]{:S(2)}) %collective-permute-start.17) | collective-permute-done | bytes 196640 | tf_op jit(solution)/shard_map/ppermute | solution.py:176
  (116 shorter events, 37.0 us)
Async XLA Ops:
  0.6 19.8 %collective-permute-start.12 = (s32[128]{0:T(128)}, s32[128]{0:T(128)}, u32[]{:S(2)}, u32[]{:S(2)}) collective-permute-start(s32[128]{0:T(128)} %bitcast.153), channel_id=1, source_target_pairs={{8,0},{16,8},{24,16},{9,1},{17,9},{25,17},{10,2},{18,10},{26,18},{... | collective-permute-start | bytes 1544 | tf_op jit(solution)/shard_map/ppermute | solution.py:172
  4.1 7.9 %collective-permute-start = (bf16[48,2048]{1,0:T(8,128)(2,1)S(1)}, bf16[48,2048]{1,0:T(8,128)(2,1)S(1)}, u32[]{:S(2)}, u32[]{:S(2)}) collective-permute-start(bf16[48,2048]{1,0:T(8,128)(2,1)S(1)} %slice.127), channel_id=1, source_target_pairs={{0,4},{4,0},{1,5},{5,1},{2,6},{6,2},{3,7},{7,3},{8,12},{12,8},{9,1... | collective-permute-start | bytes 589832 | tf_op jit(solution)/shard_map/ppermute | solution.py:176
  12.8 11.6 %collective-permute-start.1 = (bf16[48,2048]{1,0:T(8,128)(2,1)}, bf16[48,2048]{1,0:T(8,128)(2,1)}, u32[]{:S(2)}, u32[]{:S(2)}) collective-permute-start(bf16[48,2048]{1,0:T(8,128)(2,1)} %get-tuple-element.37), channel_id=1, source_target_pairs={{0,2},{1,3},{2,0},{3,1},{4,6},{5,7},{6,4},{7,5},{8,10},{9,11},{10,... | collective-permute-start | bytes 589832 | tf_op jit(solution)/shard_map/ppermute | solution.py:176
  15.6 12.1 %collective-permute-start.3 = (bf16[48,4096]{1,0:T(8,128)(2,1)}, bf16[48,4096]{1,0:T(8,128)(2,1)}, u32[]{:S(2)}, u32[]{:S(2)}) collective-permute-start(bf16[48,4096]{1,0:T(8,128)(2,1)} %get-tuple-element.35), channel_id=1, source_target_pairs={{0,2},{1,3},{2,0},{3,1},{4,6},{5,7},{6,4},{7,5},{8,10},{9,11},{10,... | collective-permute-start | bytes 1179656 | tf_op jit(solution)/shard_map/ppermute | solution.py:176
  25.4 9.8 %collective-permute-start.2 = (bf16[2,48,2048]{2,1,0:T(8,128)(2,1)S(1)}, bf16[2,48,2048]{2,1,0:T(8,128)(2,1)S(1)}, u32[]{:S(2)}, u32[]{:S(2)}) collective-permute-start(bf16[2,48,2048]{2,1,0:T(8,128)(2,1)S(1)} %pad_maximum_fusion.4), channel_id=1, source_target_pairs={{0,4},{4,0},{1,5},{5,1},{2,6},{6,2},{3,7},{7,3},{8,12},{12,8},{9,1... | collective-permute-start | bytes 1179656 | tf_op jit(solution)/shard_map/ppermute | solution.py:176
  28.8 7.7 %collective-permute-start.4 = (bf16[2,48,4096]{2,1,0:T(8,128)(2,1)S(1)}, bf16[2,48,4096]{2,1,0:T(8,128)(2,1)S(1)}, u32[]{:S(2)}, u32[]{:S(2)}) collective-permute-start(bf16[2,48,4096]{2,1,0:T(8,128)(2,1)S(1)} %pad_maximum_fusion.2), channel_id=1, source_target_pairs={{0,1},{1,0},{2,3},{3,2},{4,5},{5,4},{6,7},{7,6},{8,9},{9,8},{10,11... | collective-permute-start | bytes 2359304 | tf_op jit(solution)/shard_map/ppermute | solution.py:176
  36.4 2.4 %collective-permute-start.5 = (bf16[2,48,4096]{2,1,0:T(8,128)(2,1)S(1)}, bf16[2,48,4096]{2,1,0:T(8,128)(2,1)S(1)}, u32[]{:S(2)}, u32[]{:S(2)}) collective-permute-start(bf16[2,48,4096]{2,1,0:T(8,128)(2,1)S(1)} %pad_maximum_fusion), channel_id=1, source_target_pairs={{0,1},{1,0},{2,3},{3,2},{4,5},{5,4},{6,7},{7,6},{8,9},{9,8},{10,11... | collective-permute-start | bytes 2359304 | tf_op jit(solution)/shard_map/ppermute | solution.py:176
  39.9 7.0 %collective-permute-start.6 = (bf16[48,2048]{1,0:T(8,128)(2,1)S(1)}, bf16[48,2048]{1,0:T(8,128)(2,1)S(1)}, u32[]{:S(2)}, u32[]{:S(2)}) collective-permute-start(bf16[48,2048]{1,0:T(8,128)(2,1)S(1)} %slice.104), channel_id=1, source_target_pairs={{0,4},{4,0},{1,5},{5,1},{2,6},{6,2},{3,7},{7,3},{8,12},{12,8},{9,1... | collective-permute-start | bytes 589832 | tf_op jit(solution)/shard_map/ppermute | solution.py:176
  47.0 23.7 %collective-permute-start.7 = (bf16[48,2048]{1,0:T(8,128)(2,1)S(1)}, bf16[48,2048]{1,0:T(8,128)(2,1)S(1)}, u32[]{:S(2)}, u32[]{:S(2)}) collective-permute-start(bf16[48,2048]{1,0:T(8,128)(2,1)S(1)} %get-tuple-element.32), channel_id=1, source_target_pairs={{0,2},{1,3},{2,0},{3,1},{4,6},{5,7},{6,4},{7,5},{8,10},{9,11},{10,... | collective-permute-start | bytes 589832 | tf_op jit(solution)/shard_map/ppermute | solution.py:176
  48.6 23.6 %collective-permute-start.9 = (bf16[48,4096]{1,0:T(8,128)(2,1)S(1)}, bf16[48,4096]{1,0:T(8,128)(2,1)S(1)}, u32[]{:S(2)}, u32[]{:S(2)}) collective-permute-start(bf16[48,4096]{1,0:T(8,128)(2,1)S(1)} %get-tuple-element.30), channel_id=1, source_target_pairs={{0,2},{1,3},{2,0},{3,1},{4,6},{5,7},{6,4},{7,5},{8,10},{9,11},{10,... | collective-permute-start | bytes 1179656 | tf_op jit(solution)/shard_map/ppermute | solution.py:176
  70.7 9.8 %collective-permute-start.8 = (bf16[2,48,2048]{2,1,0:T(8,128)(2,1)S(1)}, bf16[2,48,2048]{2,1,0:T(8,128)(2,1)S(1)}, u32[]{:S(2)}, u32[]{:S(2)}) collective-permute-start(bf16[2,48,2048]{2,1,0:T(8,128)(2,1)S(1)} %pad_maximum_fusion.6), channel_id=1, source_target_pairs={{0,4},{4,0},{1,5},{5,1},{2,6},{6,2},{3,7},{7,3},{8,12},{12,8},{9,1... | collective-permute-start | bytes 1179656 | tf_op jit(solution)/shard_map/ppermute | solution.py:176
  72.3 8.5 %collective-permute-start.10 = (bf16[2,48,4096]{2,1,0:T(8,128)(2,1)S(1)}, bf16[2,48,4096]{2,1,0:T(8,128)(2,1)S(1)}, u32[]{:S(2)}, u32[]{:S(2)}) collective-permute-start(bf16[2,48,4096]{2,1,0:T(8,128)(2,1)S(1)} %pad_maximum_fusion.3), channel_id=1, source_target_pairs={{0,1},{1,0},{2,3},{3,2},{4,5},{5,4},{6,7},{7,6},{8,9},{9,8},{10,11... | collective-permute-start | bytes 2359304 | tf_op jit(solution)/shard_map/ppermute | solution.py:176
  80.7 2.4 %collective-permute-start.11 = (bf16[2,48,4096]{2,1,0:T(8,128)(2,1)S(1)}, bf16[2,48,4096]{2,1,0:T(8,128)(2,1)S(1)}, u32[]{:S(2)}, u32[]{:S(2)}) collective-permute-start(bf16[2,48,4096]{2,1,0:T(8,128)(2,1)S(1)} %pad_maximum_fusion.1), channel_id=1, source_target_pairs={{0,1},{1,0},{2,3},{3,2},{4,5},{5,4},{6,7},{7,6},{8,9},{9,8},{10,11... | collective-permute-start | bytes 2359304 | tf_op jit(solution)/shard_map/ppermute | solution.py:176
  129.9 12.7 %collective-permute-start.18 = (bf16[2,96,2048]{2,1,0:T(8,128)(2,1)S(1)}, bf16[2,96,2048]{2,1,0:T(8,128)(2,1)S(1)}, u32[]{:S(2)}, u32[]{:S(2)}) collective-permute-start(bf16[2,96,2048]{2,1,0:T(8,128)(2,1)S(1)} %slice_bitcast_fusion), channel_id=1, source_target_pairs={{0,1},{1,0},{2,3},{3,2},{4,5},{5,4},{6,7},{7,6},{8,9},{9,8},{10,11... | collective-permute-start | bytes 2359304 | tf_op jit(solution)/shard_map/ppermute | solution.py:176
  130.2 14.2 %collective-permute-start.13 = (bf16[2,96,2048]{2,1,0:T(8,128)(2,1)S(1)}, bf16[2,96,2048]{2,1,0:T(8,128)(2,1)S(1)}, u32[]{:S(2)}, u32[]{:S(2)}) collective-permute-start(bf16[2,96,2048]{2,1,0:T(8,128)(2,1)S(1)} %slice_bitcast_fusion.2), channel_id=1, source_target_pairs={{0,1},{1,0},{2,3},{3,2},{4,5},{5,4},{6,7},{7,6},{8,9},{9,8},{10,11... | collective-permute-start | bytes 2359304 | tf_op jit(solution)/shard_map/ppermute | solution.py:176
  142.9 11.2 %collective-permute-start.19 = (bf16[2,48,2048]{2,1,0:T(8,128)(2,1)S(1)}, bf16[2,48,2048]{2,1,0:T(8,128)(2,1)S(1)}, u32[]{:S(2)}, u32[]{:S(2)}) collective-permute-start(bf16[2,48,2048]{2,1,0:T(8,128)(2,1)S(1)} %broadcast_select_fusion), channel_id=1, source_target_pairs={{0,4},{4,0},{1,5},{5,1},{2,6},{6,2},{3,7},{7,3},{8,12},{12,8},{9,1... | collective-permute-start | bytes 1179656 | tf_op jit(solution)/shard_map/ppermute | solution.py:176
  144.7 26.8 %copy-start.3 = (bf16[384,4096]{1,0:T(8,128)(2,1)S(1)}, bf16[384,4096]{1,0:T(8,128)(2,1)}, u32[]{:S(2)}) copy-start(bf16[384,4096]{1,0:T(8,128)(2,1)} %copy-done.2) | copy-start | bytes 9437188
  144.7 11.1 %collective-permute-start.14 = (bf16[1,96,2048]{2,1,0:T(8,128)(2,1)S(1)}, bf16[1,96,2048]{2,1,0:T(8,128)(2,1)S(1)}, u32[]{:S(2)}, u32[]{:S(2)}) collective-permute-start(bf16[1,96,2048]{2,1,0:T(8,128)(2,1)S(1)} %slice.151), channel_id=1, source_target_pairs={{0,2},{1,3},{2,0},{3,1},{4,6},{5,7},{6,4},{7,5},{8,10},{9,11},{10,... | collective-permute-start | bytes 1179656 | tf_op jit(solution)/shard_map/ppermute | solution.py:176
  154.3 6.2 %collective-permute-start.20 = (bf16[48,2048]{1,0:T(8,128)(2,1)S(1)}, bf16[48,2048]{1,0:T(8,128)(2,1)S(1)}, u32[]{:S(2)}, u32[]{:S(2)}) collective-permute-start(bf16[48,2048]{1,0:T(8,128)(2,1)S(1)} %slice_bitcast_fusion.12), channel_id=1, source_target_pairs={{0,2},{1,3},{2,0},{3,1},{4,6},{5,7},{6,4},{7,5},{8,10},{9,11},{10,... | collective-permute-start | bytes 589832 | tf_op jit(solution)/shard_map/ppermute | solution.py:176
  156.0 5.9 %collective-permute-start.15 = (bf16[1,48,2048]{2,1,0:T(8,128)(2,1)S(1)}, bf16[1,48,2048]{2,1,0:T(8,128)(2,1)S(1)}, u32[]{:S(2)}, u32[]{:S(2)}) collective-permute-start(bf16[1,48,2048]{2,1,0:T(8,128)(2,1)S(1)} %broadcast_select_fusion.5), channel_id=1, source_target_pairs={{0,4},{4,0},{1,5},{5,1},{2,6},{6,2},{3,7},{7,3},{8,12},{12,8},{9,1... | collective-permute-start | bytes 589832 | tf_op jit(solution)/shard_map/ppermute | solution.py:176
  160.5 9.5 %collective-permute-start.21 = (bf16[48,2048]{1,0:T(8,128)(2,1)S(1)}, bf16[48,2048]{1,0:T(8,128)(2,1)S(1)}, u32[]{:S(2)}, u32[]{:S(2)}) collective-permute-start(bf16[48,2048]{1,0:T(8,128)(2,1)S(1)} %fusion.31), channel_id=1, source_target_pairs={{8,0},{16,8},{24,16},{9,1},{17,9},{25,17},{10,2},{18,10},{26,18},{... | collective-permute-start | bytes 589832 | tf_op jit(solution)/shard_map/ppermute | solution.py:172
  161.9 21.4 %collective-permute-start.16 = (bf16[48,2048]{1,0:T(8,128)(2,1)S(1)}, bf16[48,2048]{1,0:T(8,128)(2,1)S(1)}, u32[]{:S(2)}, u32[]{:S(2)}) collective-permute-start(bf16[48,2048]{1,0:T(8,128)(2,1)S(1)} %fusion.33), channel_id=1, source_target_pairs={{8,0},{16,8},{24,16},{9,1},{17,9},{25,17},{10,2},{18,10},{26,18},{... | collective-permute-start | bytes 589832 | tf_op jit(solution)/shard_map/ppermute | solution.py:172
  170.1 13.9 %collective-permute-start.22 = (bf16[48,2048]{1,0:T(8,128)(2,1)S(1)}, bf16[48,2048]{1,0:T(8,128)(2,1)S(1)}, u32[]{:S(2)}, u32[]{:S(2)}) collective-permute-start(bf16[48,2048]{1,0:T(8,128)(2,1)S(1)} %collective-permute-done.21), channel_id=1, source_target_pairs={{0,4},{4,0},{1,5},{5,1},{2,6},{6,2},{3,7},{7,3},{8,12},{12,8},{9,1... | collective-permute-start | bytes 589832 | tf_op jit(solution)/shard_map/ppermute | solution.py:176
  183.4 5.7 %collective-permute-start.17 = (bf16[48,2048]{1,0:T(8,128)(2,1)S(1)}, bf16[48,2048]{1,0:T(8,128)(2,1)S(1)}, u32[]{:S(2)}, u32[]{:S(2)}) collective-permute-start(bf16[48,2048]{1,0:T(8,128)(2,1)S(1)} %collective-permute-done.16), channel_id=1, source_target_pairs={{0,4},{4,0},{1,5},{5,1},{2,6},{6,2},{3,7},{7,3},{8,12},{12,8},{9,1... | collective-permute-start | bytes 589832 | tf_op jit(solution)/shard_map/ppermute | solution.py:176
  (9 other events, 88.5 us)
where the time goes:
time: 191 us
  Pallas kernels  91 us (48%)
  waiting for transfers between devices  49 us (26%)
  starting transfers between devices  25 us (13%)
  other arithmetic  12.2 us (6%)
  local copies, waits for them, and re-layouts  8.98 us (5%)
  matrix products  3.08 us (2%)
    pallas_call x7, Pallas kernels, call(): pl.pallas_call(kernel, name=name, grid=(grid,), in_specs=ins, out_shape=s...  91 us
    ppermute x20, waiting for transfers between devices, swap(): lax.ppermute(array, axis, [(i, i ^ bit) for i in range(lax.axis_size(axis...  42.1 us
    ppermute x20, starting transfers between devices, swap(): lax.ppermute(array, axis, [(i, i ^ bit) for i in range(lax.axis_size(axis...  21 us
    ppermute x3, waiting for transfers between devices, shifted(): return lax.ppermute(array, axis, pairs)  6.85 us
    ppermute x3, starting transfers between devices, shifted(): return lax.ppermute(array, axis, pairs)  4.01 us
  transfers between devices with their start and end apart: 23, of which 11 were waited for; matrix products, arithmetic and copies ran while one was open for 11% of the time, Pallas kernels for 23%

commit v1 on v0

v1 whole, which is shorter than its diff:
```python
import jax
import jax.numpy as jnp
from jax import lax
from jax.experimental import pallas as pl
from jax.experimental.pallas import tpu as pltpu
from jax.sharding import PartitionSpec as P

CAP = 96
EDGE = 128
SUB = 16
VMEM = 44 * 1024 * 1024


def dot(left, right, left_dim, right_dim):
    return lax.dot_general(
        left,
        right,
        (((left_dim,), (right_dim,)), ((), ())),
        preferred_element_type=jnp.float32,
    )


def masked(values, mask):
    blocks, _, cols = mask.shape
    split = values.reshape(blocks, EDGE // SUB, SUB, cols)
    return (split * mask[:, None]).reshape(blocks * EDGE, cols)


def forward_kernel(tokens, weight, mask, out):
    out[...] = dot(tokens[...], masked(weight[...], mask[...]), 1, 0)


def middle_kernel(cot, down, down_mask, gate_pre, up_pre, hidden, grad_gate_pre, grad_up_pre):
    grad_hidden = dot(cot[...], masked(down[...], down_mask[...]), 1, 1)
    pre, up = gate_pre[...], up_pre[...]
    sigmoid = jax.nn.sigmoid(pre)
    silu = pre * sigmoid
    hidden[...] = (silu * up).astype(jnp.bfloat16)
    grad_gate_pre[...] = (grad_hidden * up * sigmoid * (1.0 + pre * (1.0 - sigmoid))).astype(
        jnp.bfloat16
    )
    grad_up_pre[...] = (grad_hidden * silu).astype(jnp.bfloat16)


def input_kernel(grad_gate_pre, grad_up_pre, gate, up, gate_mask, up_mask, out):
    total = dot(grad_gate_pre[...], masked(gate[...], gate_mask[...]), 1, 1)
    total += dot(grad_up_pre[...], masked(up[...], up_mask[...]), 1, 1)
    out[...] = total.astype(jnp.bfloat16)


def outer_kernel(left, right, mask, out, flag):
    flag[...] = jnp.zeros_like(flag)
    cols = right.shape[1]
    step = min(cols, 512)
    flipped = left[...].T
    for start in range(0, cols, step):
        part = pl.ds(start, step)
        product = dot(flipped, right[:, part], 1, 0).astype(jnp.bfloat16)
        out[:, part] = masked(product, mask[:, :, part])


def call(kernel, name, grid, ins, outs, flops, args, behind=(), into=None):
    moved = sum(a.size * a.dtype.itemsize for a in args) + sum(
        s.size * s.dtype.itemsize for s, _ in outs
    )
    single = len(outs) == 1
    shapes = [s for s, _ in outs]
    specs = [b for _, b in outs]
    used = len(args)
    others = ([] if into is None else [into]) + list(behind)

    def body(*refs):
        kernel(*refs[:used], *refs[used + len(others):])

    return pl.pallas_call(
        body,
        name=name,
        grid=(grid,),
        in_specs=ins + [pl.BlockSpec(memory_space=pl.ANY)] * len(others),
        input_output_aliases={} if into is None else {used: 0},
        out_shape=shapes[0] if single else shapes,
        out_specs=specs[0] if single else specs,
        compiler_params=pltpu.CompilerParams(vmem_limit_bytes=VMEM),
        cost_estimate=pl.CostEstimate(flops=flops, bytes_accessed=moved, transcendentals=0),
    )(*args, *others)


def whole_of(array):
    return pl.BlockSpec(array.shape, lambda i: (0,) * array.ndim)


def forward(tokens, weight, mask, name, behind=()):
    rows, width = tokens.shape
    units = weight.shape[1]
    tile = min(256, units)
    out = (
        jax.ShapeDtypeStruct((rows, units), jnp.float32),
        pl.BlockSpec((rows, tile), lambda i: (0, i)),
    )
    return call(
        forward_kernel, name, units // tile,
        [
            whole_of(tokens),
            pl.BlockSpec((width, tile), lambda i: (0, i)),
            pl.BlockSpec((width // EDGE, SUB, tile), lambda i: (0, 0, i)),
        ],
        [out], 2 * rows * width * units, (tokens, weight, mask), behind,
    )


def middle(cot, down, down_mask, gate_pre, up_pre):
    rows, width = cot.shape
    units = down.shape[0]
    tile = min(256, units)
    columns = pl.BlockSpec((rows, tile), lambda i: (0, i))
    out = (jax.ShapeDtypeStruct((rows, units), jnp.bfloat16), columns)
    return call(
        middle_kernel, "middle", units // tile,
        [
            whole_of(cot),
            pl.BlockSpec((tile, width), lambda i: (i, 0)),
            pl.BlockSpec((tile // EDGE, SUB, width), lambda i: (i, 0, 0)),
            columns,
            columns,
        ],
        [out, out, out],
        2 * rows * width * units, (cot, down, down_mask, gate_pre, up_pre),
    )


def input_part(grad_gate_pre, grad_up_pre, gate, up, gate_mask, up_mask, part, parts, behind=()):
    rows, units = grad_gate_pre.shape
    width = gate.shape[0] // parts
    tile = min(512, width)
    first = part * width // tile
    weight = pl.BlockSpec((tile, units), lambda i: (i + first, 0))
    mask = pl.BlockSpec((tile // EDGE, SUB, units), lambda i: (i + first, 0, 0))
    out = (
        jax.ShapeDtypeStruct((rows, width), jnp.bfloat16),
        pl.BlockSpec((rows, tile), lambda i: (0, i)),
    )
    return call(
        input_kernel, "input_part", width // tile,
        [whole_of(grad_gate_pre), whole_of(grad_up_pre), weight, weight, mask, mask], [out],
        4 * rows * width * units,
        (grad_gate_pre, grad_up_pre, gate, up, gate_mask, up_mask), behind,
    )


def outer(left, right, mask, name, part=0, parts=1, behind=(), into=None):
    rows, height = left.shape
    cols = right.shape[1]
    tile = max(EDGE, min(height // parts, 1024 * 1024 // cols))
    count = height // parts // tile
    first = part * count
    out = (
        jax.ShapeDtypeStruct((height, cols), jnp.bfloat16),
        pl.BlockSpec((tile, cols), lambda i: (i + first, 0)),
    )
    flag = (
        jax.ShapeDtypeStruct((8, EDGE), jnp.float32),
        pl.BlockSpec((8, EDGE), lambda i: (0, 0)),
    )
    return call(
        outer_kernel, name, count,
        [
            pl.BlockSpec((rows, tile), lambda i: (0, i + first)),
            whole_of(right),
            pl.BlockSpec((tile // EDGE, SUB, cols), lambda i: (i + first, 0, 0)),
        ],
        [out, flag], 2 * rows * height * cols // parts, (left, right, mask), behind, into,
    )


def expand(keep):
    rows, cols = keep.shape
    wide = jnp.broadcast_to(
        keep.astype(jnp.bfloat16)[:, None, :, None], (rows, SUB, cols, EDGE)
    )
    return wide.reshape(rows, SUB, cols * EDGE)


def shifted(array, axis, by):
    peers = lax.axis_size(axis)
    pairs = [(i, i + by) for i in range(peers) if 0 <= i + by < peers]
    return lax.ppermute(array, axis, pairs)


def swap(array, axis, bit):
    return lax.ppermute(array, axis, [(i, i ^ bit) for i in range(lax.axis_size(axis))])


def select_rows(noised):
    slot = jnp.cumsum(noised) - 1
    return (
        (slot[None, :] == jnp.arange(CAP)[:, None]) & (noised[None, :] > 0)
    ).astype(jnp.bfloat16)


def side_by_side(own, other):
    first = lax.axis_index("row") == 0
    return jnp.concatenate(
        [jnp.where(first, own, other), jnp.where(first, other, own)], axis=-1
    )


def gather_near(top, bottom):
    return swap(top, "row", 1), swap(bottom, "col", 2)


def gather_wide(top, bottom, top_x, bottom_y):
    return side_by_side(top, top_x), jnp.stack([bottom, bottom_y])


def gather_far(top_wide, bottom_both):
    return swap(top_wide, "col", 2), swap(bottom_both, "row", 1)


def gather_chip(top_wide, bottom_both, top_y, bottom_x):
    return jnp.concatenate(
        [jnp.stack([top_wide, top_y]), side_by_side(bottom_both, bottom_x)], axis=1
    )


def gather_all(own):
    other = swap(own, "col", 1)
    return jnp.concatenate([own[0], other[0], own[1], other[1]], axis=0)


def add(left, right):
    return (left.astype(jnp.float32) + right.astype(jnp.float32)).astype(jnp.bfloat16)


def by_row(block):
    half = block.shape[1] // 2
    first = lax.axis_index("row") == 0
    top, bottom = block[:, :half], block[:, half:]
    return jnp.where(first, top, bottom), jnp.where(first, bottom, top)


def both_rows(piece, other):
    first = lax.axis_index("row") == 0
    return jnp.concatenate([jnp.where(first, piece, other), jnp.where(first, other, piece)])


def after(array, *others):
    return lax.optimization_barrier((array, *others))[0]


def paired_device(tokens, cotangent, noised, gate, up, down, keep):
    selector = select_rows(noised)
    half = CAP // 2
    rows_of = (selector[:half], selector[half:])
    t_top, t_bottom = (dot(r, tokens, 1, 0).astype(jnp.bfloat16) for r in rows_of)
    t_near = gather_near(t_top, t_bottom)
    c_top, c_bottom = (
        dot(after(r, t_top, t_bottom), cotangent, 1, 0).astype(jnp.bfloat16) for r in rows_of
    )
    gate_keep, up_keep, down_keep = lax.optimization_barrier((*keep, t_top, t_bottom))[:3]
    gate_mask, up_mask, down_mask = expand(gate_keep), expand(up_keep), expand(down_keep.T)
    t_wide = gather_wide(t_top, t_bottom, *t_near)
    t_far = gather_far(*t_wide)
    t_chip = gather_chip(*t_wide, *t_far)
    c_top, c_bottom, _ = lax.optimization_barrier((c_top, c_bottom, t_chip))
    c_near = gather_near(c_top, c_bottom)
    all_tokens = gather_all(t_chip)
    c_wide = gather_wide(c_top, c_bottom, *c_near)
    c_far = gather_far(*c_wide)
    gate_pre = forward(all_tokens, gate, gate_mask, "gate_pre", c_wide)
    c_chip = gather_chip(*c_wide, *c_far)
    c_chip = after(c_chip, gate_pre)
    up_pre = forward(all_tokens, up, up_mask, "up_pre", (c_chip,))
    all_cot = gather_all(c_chip)
    hidden, d_gate, d_up = middle(all_cot, down, down_mask, gate_pre, up_pre)
    next_selector = select_rows(shifted(after(noised, gate_pre), "section", -1))

    def core_split(block):
        block = block.reshape(2, 2, CAP, block.shape[1])
        return block[:, 0], block[:, 1]

    left = input_part(d_gate, d_up, gate, up, gate_mask, up_mask, 0, 2)
    l_keep, l_send = core_split(left)
    l_got = swap(l_send, "col", 1)
    right = input_part(d_gate, d_up, gate, up, gate_mask, up_mask, 1, 2, (l_send,))

    l_sum = add(l_keep, after(l_got, right))
    r_keep, r_send = core_split(right)
    l_got, r_got = swap(l_sum[1], "col", 2), swap(r_send, "col", 1)
    grad_down, done = outer(hidden, all_cot, down_mask, "grad_down", 0, 1, (l_sum, r_send))

    l_keep, l_send = by_row(add(l_sum[:1], after(l_got, done)[None]))
    r_keep, r_send = by_row(add(r_keep, after(r_got, done)))
    l_got, r_got = swap(l_send, "row", 1), swap(r_send, "row", 1)
    grad_up, done = outer(all_tokens, d_up, up_mask, "grad_up_a", 0, 2, (l_send, r_send))

    l_own = add(l_keep, after(l_got, done))[0]
    r_sum = add(r_keep, after(r_got, done))
    l_got, r_got = shifted(l_own, "section", -1), swap(r_sum[1], "col", 2)
    grad_up, done = outer(all_tokens, d_up, up_mask, "grad_up_b", 1, 2, (l_own, r_sum), grad_up)

    l_piece = after(l_got, done)
    r_own = add(r_sum[0], after(r_got, done))
    l_got, r_got = swap(l_piece, "row", 1), shifted(r_own, "section", -1)
    grad_gate, done = outer(all_tokens, d_gate, gate_mask, "grad_gate_a", 0, 2, (l_piece, r_own))

    l_block = both_rows(l_piece, after(l_got, done))
    r_piece = after(r_got, done)
    r_got = swap(r_piece, "row", 1)
    grad_gate, done = outer(
        all_tokens, d_gate, gate_mask, "grad_gate_b", 1, 2, (l_block, r_piece), grad_gate
    )
    block = jnp.concatenate([l_block, both_rows(r_piece, after(r_got, done))], axis=1)
    handoff = dot(next_selector, block, 0, 0).astype(jnp.bfloat16)
    return grad_gate[None], grad_up[None], grad_down[None], handoff[None]


def on_device(tokens, cotangent, noised, gate_weight, up_weight, down_weight, block_keep):
    rows, cols = lax.axis_size("row"), lax.axis_size("col")
    local_noised = noised[0]
    gate, up, down = gate_weight[0], up_weight[0], down_weight[0]
    masked_cot = cotangent[0] * local_noised[:, None].astype(jnp.bfloat16)
    if rows == 2 and cols == 4:
        keep = tuple(block_keep[0, i] for i in range(3))
        return paired_device(tokens[0], masked_cot, local_noised, gate, up, down, keep)
    gate_mask = expand(block_keep[0, 0])
    up_mask = expand(block_keep[0, 1])
    down_mask = expand(block_keep[0, 2].T)
    selector = select_rows(local_noised)
    next_selector = select_rows(shifted(local_noised, "section", -1))
    sent_tokens = dot(selector, tokens[0], 1, 0).astype(jnp.bfloat16)
    sent_cot = dot(selector, masked_cot, 1, 0).astype(jnp.bfloat16)

    def gather(block):
        wide = lax.all_gather(block, "row", axis=1, tiled=True)
        wide = wide.reshape(rows, CAP // rows, wide.shape[1])
        wide = lax.all_gather(wide, "col", axis=1, tiled=True)
        return wide.reshape(cols * CAP, wide.shape[2])

    all_tokens, all_cot = gather(sent_tokens), gather(sent_cot)
    gate_pre = forward(all_tokens, gate, gate_mask, "gate_pre")
    up_pre = forward(all_tokens, up, up_mask, "up_pre")
    hidden, grad_gate_pre, grad_up_pre = middle(all_cot, down, down_mask, gate_pre, up_pre)
    halves = [
        input_part(grad_gate_pre, grad_up_pre, gate, up, gate_mask, up_mask, part, 2)
        for part in range(2)
    ]
    grad_down = outer(hidden, all_cot, down_mask, "grad_down")[0]
    grad_gate = outer(all_tokens, grad_gate_pre, gate_mask, "grad_gate")[0]
    grad_up = outer(all_tokens, grad_up_pre, up_mask, "grad_up")[0]
    share = lax.psum_scatter(
        jnp.concatenate(halves, axis=1).astype(jnp.float32),
        ("row", "col"),
        scatter_dimension=0,
        tiled=True,
    ).astype(jnp.bfloat16)
    share = shifted(share, "section", -1)
    block = lax.all_gather(share, "row", axis=0, tiled=True)
    handoff = dot(next_selector, block, 0, 0).astype(jnp.bfloat16)
    return (grad_gate[None], grad_up[None], grad_down[None], handoff[None])


def solution(mesh):
    placed = (
        P("section", "col", "row"),
        P("section", "col", "row"),
        P("section", "col"),
        P("section", None, ("row", "col")),
        P("section", None, ("row", "col")),
        P("section", ("row", "col"), None),
        P("section", None, None, ("row", "col")),
    )
    return jax.shard_map(
        on_device,
        mesh=mesh,
        in_specs=placed,
        out_specs=(
            P("section", None, ("row", "col")),
            P("section", None, ("row", "col")),
            P("section", ("row", "col"), None),
            P("section", "col", None),
        ),
        check_vma=False,
    )
```

time: 191 us -> 186 us (0.974); the launches traced: 191 us -> 183 us
  waiting for transfers between devices: 49 us -> 33.6 us
  Pallas kernels: 91 us -> 98.8 us
  local copies, waits for them, and re-layouts: 8.98 us -> 15.1 us
  other arithmetic: 12.2 us -> 8 us
    ppermute x20 -> x18, waiting for transfers between devices: 42.1 us -> 33.6 us  [swap(): lax.ppermute(array, axis, [(i, i ^ bit) for i in range(lax.axis_size(axis...]
    pallas_call x7 -> x10, Pallas kernels: 91 us -> 98.8 us  [call(): pl.pallas_call(body, name=name, grid=(grid,), in_specs=ins + [pl.BlockSpe...]
    ppermute x3, waiting for transfers between devices: 6.85 us -> 0.01 us  [shifted(): return lax.ppermute(array, axis, pairs)]
    squeeze x3 -> x9, local copies, waits for them, and re-layouts: 0.15 us -> 6.53 us  [the longest x4 4.49 us: gather_all(): return jnp.concatenate([own[0], other[0], own[1], other[1]], axis=0)]
    another operation x9 -> x6, other arithmetic: 5.99 us -> 0.54 us
    unnamed x31 -> x35, local copies, waits for them, and re-layouts: 3.34 us -> 6.35 us
    convert_element_type x5, other arithmetic: 0.82 us -> 3.4 us  [add(): (left.astype(jnp.float32) + right.astype(jnp.float32)).astype(jnp.bfloat16)]
    concatenate x2 -> x5, other arithmetic: 0.11 us -> 2.03 us  [the longest x2 1.38 us: gather_chip(): jnp.concatenate([jnp.stack([top_wide, top_y]), side_by_side(bottom_both,...]
  transfers between devices with their start and end apart: 23 -> 21, of which waited for: 11 -> 10; matrix products, arithmetic and copies ran while one was open for 11% -> 7% of each run, Pallas kernels for 23% -> 30%
where the time goes in v1:
time: 186 us; the launch traced here: 183 us
  Pallas kernels  98.8 us (53%)
  waiting for transfers between devices  33.6 us (18%)
  starting transfers between devices  24.2 us (13%)
  local copies, waits for them, and re-layouts  15.1 us (8%)
  other arithmetic  8 us (4%)
  matrix products  2.44 us (1%)
    pallas_call x10, Pallas kernels, call(): pl.pallas_call(body, name=name, grid=(grid,), in_specs=ins + [pl.BlockSpe...  98.8 us
    ppermute x18, waiting for transfers between devices, swap(): lax.ppermute(array, axis, [(i, i ^ bit) for i in range(lax.axis_size(axis...  33.6 us
    ppermute x18, starting transfers between devices, swap(): lax.ppermute(array, axis, [(i, i ^ bit) for i in range(lax.axis_size(axis...  19.9 us
    unnamed x35, local copies, waits for them, and re-layouts  6.35 us
    squeeze x4, local copies, waits for them, and re-layouts, gather_all(): return jnp.concatenate([own[0], other[0], own[1], other[1]], axis=0)  4.49 us
    ppermute x3, starting transfers between devices, shifted(): return lax.ppermute(array, axis, pairs)  4.28 us
  transfers between devices with their start and end apart: 21, of which 10 were waited for; matrix products, arithmetic and copies ran while one was open for 7% of the time, Pallas kernels for 30%

profile of v1, /device:TPU:0, one launch (start us, length us, event | category | flops | bytes accessed | tf_op | source)
XLA Modules:
  0.0 183.3 jit_solution(15194706005999099376)
XLA Ops:
  2.7 3.0 %collective-permute-start = (bf16[48,2048]{1,0:T(8,128)(2,1)S(1)}, bf16[48,2048]{1,0:T(8,128)(2,1)S(1)}, u32[]{:S(2)}, u32[]{:S(2)}) collective-permute-start(bf16[48,2048]{1,0:T(8,128)(2,1)S(1)} %convolution_convert_fusion.4), channel_id=1, source_target_pairs={{0,4},{4,0},{1,5},{5,1},{2,6},{6,2},{3,7},{7,3},{8,12},{12,8},{9,1... | collective-permute-start | bytes 589832 | tf_op jit(solution)/shard_map/ppermute | solution.py:190
  10.3 2.1 %collective-permute-done.2 = bf16[48,2048]{1,0:T(8,128)(2,1)S(1)} collective-permute-done((bf16[48,2048]{1,0:T(8,128)(2,1)S(1)}, bf16[48,2048]{1,0:T(8,128)(2,1)S(1)}, u32[]{:S(2)}, u32[]{:S(2)}) %collective-permute-start.2) | collective-permute-done | bytes 196640 | tf_op jit(solution)/shard_map/ppermute | solution.py:190
  12.9 1.8 collective-permute-start.1
  14.7 7.4 %collective-permute-done.3 = bf16[2,48,2048]{2,1,0:T(8,128)(2,1)S(1)} collective-permute-done((bf16[2,48,2048]{2,1,0:T(8,128)(2,1)S(1)}, bf16[2,48,2048]{2,1,0:T(8,128)(2,1)S(1)}, u32[]{:S(2)}, u32[]{:S(2)}) %collective-permute-start.3) | collective-permute-done | bytes 393248 | tf_op jit(solution)/shard_map/ppermute | solution.py:190
  26.0 2.5 %collective-permute-done.7 = bf16[48,2048]{1,0:T(8,128)(2,1)S(1)} collective-permute-done((bf16[48,2048]{1,0:T(8,128)(2,1)S(1)}, bf16[48,2048]{1,0:T(8,128)(2,1)S(1)}, u32[]{:S(2)}, u32[]{:S(2)}) %collective-permute-start.7) | collective-permute-done | bytes 196640 | tf_op jit(solution)/shard_map/ppermute | solution.py:190
  30.0 2.2 %collective-permute-done.5 = bf16[48,2048]{1,0:T(8,128)(2,1)S(1)} collective-permute-done((bf16[48,2048]{1,0:T(8,128)(2,1)S(1)}, bf16[48,2048]{1,0:T(8,128)(2,1)S(1)}, u32[]{:S(2)}, u32[]{:S(2)}) %collective-permute-start.5) | collective-permute-done | bytes 196640 | tf_op jit(solution)/shard_map/ppermute | solution.py:190
  33.0 7.2 %collective-permute-done.8 = bf16[2,48,2048]{2,1,0:T(8,128)(2,1)S(1)} collective-permute-done((bf16[2,48,2048]{2,1,0:T(8,128)(2,1)S(1)}, bf16[2,48,2048]{2,1,0:T(8,128)(2,1)S(1)}, u32[]{:S(2)}, u32[]{:S(2)}) %collective-permute-start.8) | collective-permute-done | bytes 393248 | tf_op jit(solution)/shard_map/ppermute | solution.py:190
  40.2 2.4 %collective-permute-done.6 = bf16[48,4096]{1,0:T(8,128)(2,1)S(1)} collective-permute-done((bf16[48,4096]{1,0:T(8,128)(2,1)S(1)}, bf16[48,4096]{1,0:T(8,128)(2,1)S(1)}, u32[]{:S(2)}, u32[]{:S(2)}) %collective-permute-start.6) | collective-permute-done | bytes 393248 | tf_op jit(solution)/shard_map/ppermute | solution.py:190
  44.5 13.4 %gate_pre.1.refs_3_ = f32[384,2048]{1,0:T(8,128)S(1)} custom-call(bf16[384,4096]{1,0:T(8,128)(2,1)S(1)} %pad_maximum_fusion.refs_0_, bf16[4096,2048]{1,0:T(8,128)(2,1)} %bitcast.111, bf16[32,16,2048]{2,1,0:T(8,128)(2,1)S(1)} %broadcast_in_dim.50.refs_2_.refs_4_, bf16[48,4096]{1,0:T(8,128)(2,1)S(1)} %get-tuple-element.81.refs_3_, ...), custom_call_target="tpu_custom_call" | custom-call | flops 6442450944 | bytes 25165824 | tf_op jit(solution)/shard_map/gate_pre/pallas_call | solution.py:75
  59.5 2.7 %slice_bitcast_fusion.11 = (bf16[96,4096]{1,0:T(8,128)(2,1)}, bf16[96,4096]{1,0:T(8,128)(2,1)}) fusion(bf16[2,96,4096]{2,1,0:T(8,128)(2,1)} %maximum_maximum_fusion.1.refs_3_), kind=kLoop, calls=%fused_computation.35 | loop fusion | bytes 3145728 | tf_op jit(solution)/shard_map/squeeze | solution.py:227
  62.5 12.5 %up_pre.1.refs_4_ = f32[384,2048]{1,0:T(8,128)S(1)} custom-call(bf16[384,4096]{1,0:T(8,128)(2,1)S(1)} %pad_maximum_fusion.refs_0_, bf16[4096,2048]{1,0:T(8,128)(2,1)} %bitcast.114, bf16[32,16,2048]{2,1,0:T(8,128)(2,1)S(1)} %broadcast_in_dim.56.refs_2_.refs_5_, bf16[2,96,4096]{2,1,0:T(8,128)(2,1)} %maximum_maximum_fusion.1.refs_3_), custom_call_target="tpu_custom_call" | custom-call | flops 6442450944 | bytes 25165824 | tf_op jit(solution)/shard_map/up_pre/pallas_call | solution.py:75
  75.1 1.7 copy-done.9
  79.5 13.3 %middle.1 = (bf16[384,2048]{1,0:T(8,128)(2,1)S(1)}, bf16[384,2048]{1,0:T(8,128)(2,1)S(1)}, bf16[384,2048]{1,0:T(8,128)(2,1)S(1)}) custom-call(bf16[384,4096]{1,0:T(8,128)(2,1)S(1)} %pad_maximum_fusion.1.refs_0_.refs_1_, bf16[2048,4096]{1,0:T(8,128)(2,1)} %bitcast.117, bf16[16,16,4096]{2,1,0:T(8,128)(2,1)S(1)} %broadcast_in_dim.53.refs_2_, ...), custom_call_target="tpu_custom_call" | custom-call | flops 6442450944 | bytes 33030144 | tf_op jit(solution)/shard_map/middle/pallas_call | solution.py:75
  93.9 10.1 %input_part.2 = bf16[384,2048]{1,0:T(8,128)(2,1)S(1)} custom-call(bf16[384,2048]{1,0:T(8,128)(2,1)S(1)} %get-tuple-element.42.refs_0_.refs_1_, bf16[384,2048]{1,0:T(8,128)(2,1)S(1)} %get-tuple-element.43.refs_1_, bf16[4096,2048]{1,0:T(8,128)(2,1)} %bitcast.112, bf16[4096,2048]{1,0:T(8,128)(2,1)} %bitcast.115, bf16[32,16,2048]{2,1,0:T(8,128)(2,1)S(1)} %copy-done.5, ...), custom_call_target="tpu_custom_call" | custom-call | flops 6442450944 | bytes 42467328 | tf_op jit(solution)/shard_map/input_part/pallas_call | solution.py:75
  104.7 11.0 %input_part.3 = bf16[384,2048]{1,0:T(8,128)(2,1)} custom-call(bf16[384,2048]{1,0:T(8,128)(2,1)S(1)} %get-tuple-element.42.refs_0_.refs_1_, bf16[384,2048]{1,0:T(8,128)(2,1)S(1)} %get-tuple-element.43.refs_1_, bf16[4096,2048]{1,0:T(8,128)(2,1)} %bitcast.113, bf16[4096,2048]{1,0:T(8,128)(2,1)} %bitcast.116, bf16[32,16,2048]{2,1,0:T(8,128)(2,1)S(1)} %copy-done.5, ...), custom_call_target="tpu_custom_call" | custom-call | flops 6442450944 | bytes 42467328 | tf_op jit(solution)/shard_map/input_part/pallas_call | solution.py:75
  120.5 11.9 %grad_down.1 = (bf16[2048,4096]{1,0:T(8,128)(2,1)}, f32[8,128]{1,0:T(8,128)}) custom-call(bf16[384,2048]{1,0:T(8,128)(2,1)S(1)} %copy-done.11, bf16[384,4096]{1,0:T(8,128)(2,1)S(1)} %pad_maximum_fusion.1.refs_0_.refs_1_, bf16[16,16,4096]{2,1,0:T(8,128)(2,1)S(1)} %broadcast_in_dim.53.refs_2_, bf16[2,96,2048]{2,1,0:T(8,128)(2,1)S(1)} %fusion.2.refs_3_, ...), custom_call_target="tpu_custom_call" | custom-call | flops 6442450944 | bytes 23597056 | tf_op jit(solution)/shard_map/grad_down/pallas_call | solution.py:75
  136.4 6.7 %grad_up_a.1 = (bf16[4096,2048]{1,0:T(8,128)(2,1)}, f32[8,128]{1,0:T(8,128)}) custom-call(bf16[384,4096]{1,0:T(8,128)(2,1)S(1)} %pad_maximum_fusion.refs_0_, bf16[384,2048]{1,0:T(8,128)(2,1)S(1)} %get-tuple-element.43.refs_1_, bf16[32,16,2048]{2,1,0:T(8,128)(2,1)S(1)} %copy-done.7, bf16[1,48,2048]{2,1,0:T(8,128)(2,1)S(1)} %broadcast_select_fusion.5.refs_3_, ...), custom_call_target="tpu_custom_call" | custom-call | flops 3221225472 | bytes 23597056 | tf_op jit(solution)/shard_map/grad_up_a/pallas_call | solution.py:75
  143.1 3.1 %collective-permute-done.15 = bf16[2,48,2048]{2,1,0:T(8,128)(2,1)S(1)} collective-permute-done((bf16[2,48,2048]{2,1,0:T(8,128)(2,1)S(1)}, bf16[2,48,2048]{2,1,0:T(8,128)(2,1)S(1)}, u32[]{:S(2)}, u32[]{:S(2)}) %collective-permute-start.15) | collective-permute-done | bytes 393248 | tf_op jit(solution)/shard_map/ppermute | solution.py:190
  147.8 1.8 collective-permute-done.12
  151.0 6.7 %grad_up_b.1 = (bf16[4096,2048]{1,0:T(8,128)(2,1)}, f32[8,128]{1,0:T(8,128)}) custom-call(bf16[384,4096]{1,0:T(8,128)(2,1)S(1)} %pad_maximum_fusion.refs_0_, bf16[384,2048]{1,0:T(8,128)(2,1)S(1)} %get-tuple-element.43.refs_1_, bf16[32,16,2048]{2,1,0:T(8,128)(2,1)S(1)} %copy-done.7, ...), custom_call_target="tpu_custom_call", output_to_operand_aliasing={{0}: (3, {})} | custom-call | flops 3221225472 | bytes 23597056 | tf_op jit(solution)/shard_map/grad_up_b/pallas_call | solution.py:75
  160.7 6.6 %grad_gate_a.1 = (bf16[4096,2048]{1,0:T(8,128)(2,1)}, f32[8,128]{1,0:T(8,128)}) custom-call(bf16[384,4096]{1,0:T(8,128)(2,1)S(1)} %pad_maximum_fusion.refs_0_, bf16[384,2048]{1,0:T(8,128)(2,1)S(1)} %get-tuple-element.42.refs_0_.refs_1_, bf16[32,16,2048]{2,1,0:T(8,128)(2,1)S(1)} %copy-done.5, bf16[48,2048]{1,0:T(8,128)(2,1)S(1)} %collective-permute-done.14.refs_3_, ...), custom_call_target="tpu_custom_call" | custom-call | flops 3221225472 | bytes 23597056 | tf_op jit(solution)/shard_map/grad_gate_a/pallas_call | solution.py:75
  168.8 4.5 %collective-permute-done.20 = bf16[48,2048]{1,0:T(8,128)(2,1)S(1)} collective-permute-done((bf16[48,2048]{1,0:T(8,128)(2,1)S(1)}, bf16[48,2048]{1,0:T(8,128)(2,1)S(1)}, u32[]{:S(2)}, u32[]{:S(2)}) %collective-permute-start.20) | collective-permute-done | bytes 196640 | tf_op jit(solution)/shard_map/ppermute | solution.py:190
  173.3 1.9 %copy-done.3 = bf16[384,4096]{1,0:T(8,128)(2,1)S(1)} copy-done((bf16[384,4096]{1,0:T(8,128)(2,1)S(1)}, bf16[384,4096]{1,0:T(8,128)(2,1)}, u32[]{:S(2)}) %copy-start.3) | copy-done | bytes 3145752
  175.2 6.6 %grad_gate_b.1 = (bf16[4096,2048]{1,0:T(8,128)(2,1)}, f32[8,128]{1,0:T(8,128)}) custom-call(bf16[384,4096]{1,0:T(8,128)(2,1)S(1)} %copy-done.3, bf16[384,2048]{1,0:T(8,128)(2,1)S(1)} %get-tuple-element.42.refs_0_.refs_1_, bf16[32,16,2048]{2,1,0:T(8,128)(2,1)S(1)} %copy-done.5, ...), custom_call_target="tpu_custom_call", output_to_operand_aliasing={{0}: (3, {})} | custom-call | flops 3221225472 | bytes 23597056 | tf_op jit(solution)/shard_map/grad_gate_b/pallas_call | solution.py:75
  (122 shorter events, 39.1 us)
Async XLA Ops:
  2.7 10.1 %collective-permute-start = (bf16[48,2048]{1,0:T(8,128)(2,1)S(1)}, bf16[48,2048]{1,0:T(8,128)(2,1)S(1)}, u32[]{:S(2)}, u32[]{:S(2)}) collective-permute-start(bf16[48,2048]{1,0:T(8,128)(2,1)S(1)} %convolution_convert_fusion.4), channel_id=1, source_target_pairs={{0,4},{4,0},{1,5},{5,1},{2,6},{6,2},{3,7},{7,3},{8,12},{12,8},{9,1... | collective-permute-start | bytes 589832 | tf_op jit(solution)/shard_map/ppermute | solution.py:190
  5.9 6.4 %collective-permute-start.2 = (bf16[48,2048]{1,0:T(8,128)(2,1)S(1)}, bf16[48,2048]{1,0:T(8,128)(2,1)S(1)}, u32[]{:S(2)}, u32[]{:S(2)}) collective-permute-start(bf16[48,2048]{1,0:T(8,128)(2,1)S(1)} %convolution_convert_fusion.3), channel_id=1, source_target_pairs={{0,2},{1,3},{2,0},{3,1},{4,6},{5,7},{6,4},{7,5},{8,10},{9,11},{10,... | collective-permute-start | bytes 589832 | tf_op jit(solution)/shard_map/ppermute | solution.py:190
  12.4 9.7 %collective-permute-start.3 = (bf16[2,48,2048]{2,1,0:T(8,128)(2,1)S(1)}, bf16[2,48,2048]{2,1,0:T(8,128)(2,1)S(1)}, u32[]{:S(2)}, u32[]{:S(2)}) collective-permute-start(bf16[2,48,2048]{2,1,0:T(8,128)(2,1)S(1)} %pad_maximum_fusion.3), channel_id=1, source_target_pairs={{0,4},{4,0},{1,5},{5,1},{2,6},{6,2},{3,7},{7,3},{8,12},{12,8},{9,1... | collective-permute-start | bytes 1179656 | tf_op jit(solution)/shard_map/ppermute | solution.py:190
  12.9 9.8 %collective-permute-start.1 = (bf16[48,4096]{1,0:T(8,128)(2,1)S(1)}, bf16[48,4096]{1,0:T(8,128)(2,1)S(1)}, u32[]{:S(2)}, u32[]{:S(2)}) collective-permute-start(bf16[48,4096]{1,0:T(8,128)(2,1)S(1)} %get-tuple-element.85), channel_id=1, source_target_pairs={{0,2},{1,3},{2,0},{3,1},{4,6},{5,7},{6,4},{7,5},{8,10},{9,11},{10,... | collective-permute-start | bytes 1179656 | tf_op jit(solution)/shard_map/ppermute | solution.py:190
  22.8 5.7 %collective-permute-start.7 = (bf16[48,2048]{1,0:T(8,128)(2,1)S(1)}, bf16[48,2048]{1,0:T(8,128)(2,1)S(1)}, u32[]{:S(2)}, u32[]{:S(2)}) collective-permute-start(bf16[48,2048]{1,0:T(8,128)(2,1)S(1)} %convolution_convert_fusion.1), channel_id=1, source_target_pairs={{0,2},{1,3},{2,0},{3,1},{4,6},{5,7},{6,4},{7,5},{8,10},{9,11},{10,... | collective-permute-start | bytes 589832 | tf_op jit(solution)/shard_map/ppermute | solution.py:190
  24.4 19.5 %collective-permute-start.4 = (bf16[2,96,4096]{2,1,0:T(8,128)(2,1)S(1)}, bf16[2,96,4096]{2,1,0:T(8,128)(2,1)S(1)}, u32[]{:S(2)}, u32[]{:S(2)}) collective-permute-start(bf16[2,96,4096]{2,1,0:T(8,128)(2,1)S(1)} %maximum_maximum_fusion), channel_id=1, source_target_pairs={{0,1},{1,0},{2,3},{3,2},{4,5},{5,4},{6,7},{7,6},{8,9},{9,8},{10,11... | collective-permute-start | bytes 4718600 | tf_op jit(solution)/shard_map/ppermute | solution.py:190
  24.4 7.8 %collective-permute-start.5 = (bf16[48,2048]{1,0:T(8,128)(2,1)S(1)}, bf16[48,2048]{1,0:T(8,128)(2,1)S(1)}, u32[]{:S(2)}, u32[]{:S(2)}) collective-permute-start(bf16[48,2048]{1,0:T(8,128)(2,1)S(1)} %convolution_convert_fusion.2), channel_id=1, source_target_pairs={{0,4},{4,0},{1,5},{5,1},{2,6},{6,2},{3,7},{7,3},{8,12},{12,8},{9,1... | collective-permute-start | bytes 589832 | tf_op jit(solution)/shard_map/ppermute | solution.py:190
  28.5 11.6 %collective-permute-start.8 = (bf16[2,48,2048]{2,1,0:T(8,128)(2,1)S(1)}, bf16[2,48,2048]{2,1,0:T(8,128)(2,1)S(1)}, u32[]{:S(2)}, u32[]{:S(2)}) collective-permute-start(bf16[2,48,2048]{2,1,0:T(8,128)(2,1)S(1)} %pad_maximum_fusion.5.refs_4_), channel_id=1, source_target_pairs={{0,4},{4,0},{1,5},{5,1},{2,6},{6,2},{3,7},{7,3},{8,12},{12,8},{9,1... | collective-permute-start | bytes 1179656 | tf_op jit(solution)/shard_map/ppermute | solution.py:190
  32.3 10.3 %collective-permute-start.6 = (bf16[48,4096]{1,0:T(8,128)(2,1)S(1)}, bf16[48,4096]{1,0:T(8,128)(2,1)S(1)}, u32[]{:S(2)}, u32[]{:S(2)}) collective-permute-start(bf16[48,4096]{1,0:T(8,128)(2,1)S(1)} %get-tuple-element.81.refs_3_), channel_id=1, source_target_pairs={{0,2},{1,3},{2,0},{3,1},{4,6},{5,7},{6,4},{7,5},{8,10},{9,11},{10,... | collective-permute-start | bytes 1179656 | tf_op jit(solution)/shard_map/ppermute | solution.py:190
  44.3 116.5 %copy-start.2 = (bf16[384,4096]{1,0:T(8,128)(2,1)}, bf16[384,4096]{1,0:T(8,128)(2,1)S(1)}, u32[]{:S(2)}) copy-start(bf16[384,4096]{1,0:T(8,128)(2,1)S(1)} %pad_maximum_fusion.refs_0_) | copy-start | bytes 9437188
  57.9 17.1 %copy-start.8 = (f32[384,2048]{1,0:T(8,128)}, f32[384,2048]{1,0:T(8,128)S(1)}, u32[]{:S(2)}) copy-start(f32[384,2048]{1,0:T(8,128)S(1)} %gate_pre.1.refs_3_) | copy-start | bytes 9437188
  58.0 18.7 %collective-permute-start.19 = (s32[128]{0:T(128)S(1)}, s32[128]{0:T(128)S(1)}, u32[]{:S(2)}, u32[]{:S(2)}) collective-permute-start(s32[128]{0:T(128)S(1)} %bitcast.137), channel_id=1, source_target_pairs={{8,0},{16,8},{24,16},{9,1},{17,9},{25,17},{10,2},{18,10},{26,18},{... | collective-permute-start | bytes 1544 | tf_op jit(solution)/shard_map/ppermute | solution.py:186
  59.4 17.7 %collective-permute-start.9 = (bf16[2,96,4096]{2,1,0:T(8,128)(2,1)}, bf16[2,96,4096]{2,1,0:T(8,128)(2,1)}, u32[]{:S(2)}, u32[]{:S(2)}) collective-permute-start(bf16[2,96,4096]{2,1,0:T(8,128)(2,1)} %maximum_maximum_fusion.1.refs_3_), channel_id=1, source_target_pairs={{0,1},{1,0},{2,3},{3,2},{4,5},{5,4},{6,7},{7,6},{8,9},{9,8},{10,11... | collective-permute-start | bytes 4718600 | tf_op jit(solution)/shard_map/ppermute | solution.py:190
  79.4 14.5 %copy-start.5 = (bf16[32,16,2048]{2,1,0:T(8,128)(2,1)S(1)}, bf16[32,16,2048]{2,1,0:T(8,128)(2,1)}, u32[]{:S(2)}) copy-start(bf16[32,16,2048]{2,1,0:T(8,128)(2,1)} %copy-done.4) | copy-start | bytes 6291460
  104.1 12.9 %collective-permute-start.10 = (bf16[2,96,2048]{2,1,0:T(8,128)(2,1)S(1)}, bf16[2,96,2048]{2,1,0:T(8,128)(2,1)}, u32[]{:S(2)}, u32[]{:S(2)}) collective-permute-start(bf16[2,96,2048]{2,1,0:T(8,128)(2,1)S(1)} %slice_bitcast_fusion.2.refs_6_), channel_id=1, source_target_pairs={{0,1},{1,0},{2,3},{3,2},{4,5},{5,4},{6,7},{7,6},{8,9},{9,8},{10,11... | collective-permute-start | bytes 2359304 | tf_op jit(solution)/shard_map/ppermute | solution.py:190
  116.8 15.6 %collective-permute-start.13 = (bf16[2,96,2048]{2,1,0:T(8,128)(2,1)S(1)}, bf16[2,96,2048]{2,1,0:T(8,128)(2,1)}, u32[]{:S(2)}, u32[]{:S(2)}) collective-permute-start(bf16[2,96,2048]{2,1,0:T(8,128)(2,1)S(1)} %slice_bitcast_fusion.1.refs_4_), channel_id=1, source_target_pairs={{0,1},{1,0},{2,3},{3,2},{4,5},{5,4},{6,7},{7,6},{8,9},{9,8},{10,11... | collective-permute-start | bytes 2359304 | tf_op jit(solution)/shard_map/ppermute | solution.py:190
  118.5 17.1 %collective-permute-start.11 = (bf16[96,2048]{1,0:T(8,128)(2,1)S(1)}, bf16[96,2048]{1,0:T(8,128)(2,1)S(1)}, u32[]{:S(2)}, u32[]{:S(2)}) collective-permute-start(bf16[96,2048]{1,0:T(8,128)(2,1)S(1)} %slice_bitcast_fusion.12), channel_id=1, source_target_pairs={{0,2},{1,3},{2,0},{3,1},{4,6},{5,7},{6,4},{7,5},{8,10},{9,11},{10,... | collective-permute-start | bytes 1179656 | tf_op jit(solution)/shard_map/ppermute | solution.py:190
  134.1 12.0 %collective-permute-start.15 = (bf16[2,48,2048]{2,1,0:T(8,128)(2,1)S(1)}, bf16[2,48,2048]{2,1,0:T(8,128)(2,1)S(1)}, u32[]{:S(2)}, u32[]{:S(2)}) collective-permute-start(bf16[2,48,2048]{2,1,0:T(8,128)(2,1)S(1)} %broadcast_select_fusion.refs_4_), channel_id=1, source_target_pairs={{0,4},{4,0},{1,5},{5,1},{2,6},{6,2},{3,7},{7,3},{8,12},{12,8},{9,1... | collective-permute-start | bytes 1179656 | tf_op jit(solution)/shard_map/ppermute | solution.py:190
  135.7 13.9 %collective-permute-start.12 = (bf16[1,48,2048]{2,1,0:T(8,128)(2,1)S(1)}, bf16[1,48,2048]{2,1,0:T(8,128)(2,1)S(1)}, u32[]{:S(2)}, u32[]{:S(2)}) collective-permute-start(bf16[1,48,2048]{2,1,0:T(8,128)(2,1)S(1)} %broadcast_select_fusion.5.refs_3_), channel_id=1, source_target_pairs={{0,4},{4,0},{1,5},{5,1},{2,6},{6,2},{3,7},{7,3},{8,12},{12,8},{9,1... | collective-permute-start | bytes 589832 | tf_op jit(solution)/shard_map/ppermute | solution.py:190
  146.3 11.3 %collective-permute-start.16 = (bf16[48,2048]{1,0:T(8,128)(2,1)S(1)}, bf16[48,2048]{1,0:T(8,128)(2,1)S(1)}, u32[]{:S(2)}, u32[]{:S(2)}) collective-permute-start(bf16[48,2048]{1,0:T(8,128)(2,1)S(1)} %slice_bitcast_fusion.13), channel_id=1, source_target_pairs={{0,2},{1,3},{2,0},{3,1},{4,6},{5,7},{6,4},{7,5},{8,10},{9,11},{10,... | collective-permute-start | bytes 589832 | tf_op jit(solution)/shard_map/ppermute | solution.py:190
  149.7 9.5 %collective-permute-start.14 = (bf16[48,2048]{1,0:T(8,128)(2,1)S(1)}, bf16[48,2048]{1,0:T(8,128)(2,1)S(1)}, u32[]{:S(2)}, u32[]{:S(2)}) collective-permute-start(bf16[48,2048]{1,0:T(8,128)(2,1)S(1)} %fusion.16.refs_4_), channel_id=1, source_target_pairs={{8,0},{16,8},{24,16},{9,1},{17,9},{25,17},{10,2},{18,10},{26,18},{... | collective-permute-start | bytes 589832 | tf_op jit(solution)/shard_map/ppermute | solution.py:186
  157.7 9.6 %collective-permute-start.18 = (bf16[48,2048]{1,0:T(8,128)(2,1)S(1)}, bf16[48,2048]{1,0:T(8,128)(2,1)S(1)}, u32[]{:S(2)}, u32[]{:S(2)}) collective-permute-start(bf16[48,2048]{1,0:T(8,128)(2,1)S(1)} %fusion.13.refs_4_), channel_id=1, source_target_pairs={{8,0},{16,8},{24,16},{9,1},{17,9},{25,17},{10,2},{18,10},{26,18},{... | collective-permute-start | bytes 589832 | tf_op jit(solution)/shard_map/ppermute | solution.py:186
  159.3 9.5 %collective-permute-start.17 = (bf16[48,2048]{1,0:T(8,128)(2,1)S(1)}, bf16[48,2048]{1,0:T(8,128)(2,1)S(1)}, u32[]{:S(2)}, u32[]{:S(2)}) collective-permute-start(bf16[48,2048]{1,0:T(8,128)(2,1)S(1)} %collective-permute-done.14.refs_3_), channel_id=1, source_target_pairs={{0,4},{4,0},{1,5},{5,1},{2,6},{6,2},{3,7},{7,3},{8,12},{12,8},{9,1... | collective-permute-start | bytes 589832 | tf_op jit(solution)/shard_map/ppermute | solution.py:190
  167.4 5.9 %collective-permute-start.20 = (bf16[48,2048]{1,0:T(8,128)(2,1)S(1)}, bf16[48,2048]{1,0:T(8,128)(2,1)S(1)}, u32[]{:S(2)}, u32[]{:S(2)}) collective-permute-start(bf16[48,2048]{1,0:T(8,128)(2,1)S(1)} %collective-permute-done.18.refs_5_), channel_id=1, source_target_pairs={{0,4},{4,0},{1,5},{5,1},{2,6},{6,2},{3,7},{7,3},{8,12},{12,8},{9,1... | collective-permute-start | bytes 589832 | tf_op jit(solution)/shard_map/ppermute | solution.py:190
  (13 other events, 82.6 us)
